TPU v7x, 32 devices: a whole 2x2x4 slice. The times are simulated.
32 devices in a mesh: seq: 8 (over z, x), tensor: 4 (over y, core).
Axes of the slice: x: 2, y: 2, z: 4, core: 2. Of those that a mesh axis runs over, the one named last changes fastest.
Arguments:
- queries: bfloat16 [7168, 2048], P('seq', 'tensor'), may hold values from -256 to 256
- db_states: bfloat16 [128, 64, 896], P('seq', None, 'tensor'), may hold values from -4096 to 4096
- enc_gain: float32 [896], replicated, may hold values from 0.1 to 1.9
- kv_weight: bfloat16 [896, 2, 2048], P(None, None, 'tensor'), may hold values from -0.1875 to 0.1875
- shard_ids: int32 [112, 2], P('seq'), may hold values from 0 to 7, as said below
- offsets: int32 [112, 2], P('seq'), may hold values from 0 to 14
Outputs:
- attention_out: bfloat16 [7168, 2048], P('seq', 'tensor')
Inputs may be any that keep to these rules, and one draw needn't show every extreme that they name: `shard_ids`: the neighbours named by the 14 groups of one device lie at most 4 in any one shard, and some shard is named exactly 4 times by the groups of every device.
All inputs are finite; a program needn't handle non-finite values.
Results may differ from a plain program's by a relative error of at most 0.0087.
Values may be sent and summed in bfloat16 or wider, within the bound.
A program may use at most 64 MiB of HBM per device.

v0:
```python
import math
import jax
import jax.numpy as jnp
from jax import lax
from jax.sharding import PartitionSpec as P

HEAD_DIM = 128
epsilon = 1e-06


def passed_along(block, axis, distance):
    devices = range(lax.axis_size(axis))
    route = [(i - distance, i) for i in devices if i - distance in devices]
    return lax.ppermute(block, axis, route)


def attend(query_win, kv_win):
    scores = jnp.einsum(
        "wqhd,wkhd->whqk", query_win, kv_win[:, :, 0], preferred_element_type=jnp.float32
    ) / math.sqrt(HEAD_DIM)
    highest = jnp.max(scores, axis=-1, keepdims=True)
    expo = jnp.exp(scores - highest)
    weights = (expo / jnp.sum(expo, axis=-1, keepdims=True)).astype(jnp.bfloat16)
    mixed = jnp.einsum(
        "whqk,wkhd->wqhd", weights, kv_win[:, :, 1], preferred_element_type=jnp.float32
    ).astype(jnp.bfloat16)
    return mixed.reshape(query_win.shape[0] * query_win.shape[1], -1)


def per_device(queries, db_states, enc_gain, kv_weight, shard_ids, offsets):
    seq_count = lax.axis_size("seq")
    group_count = shard_ids.shape[0]
    neigh_count = 2 * group_count
    slot_cap = (neigh_count + seq_count - 1) // seq_count
    group_len = db_states.shape[1]
    enc_width = kv_weight.shape[0]
    head_count = kv_weight.shape[2] // HEAD_DIM
    tok_count = queries.shape[0]
    query_cols = queries.shape[1]
    projection = kv_weight.reshape(enc_width, -1)
    token_rows = neigh_count * 2 * group_len
    neigh_shard = shard_ids.reshape(neigh_count)
    neigh_offset = offsets.reshape(neigh_count)
    owners = jnp.arange(seq_count, dtype=jnp.int32)
    onehot = (neigh_shard[:, None] == owners[None, :]).astype(jnp.int32)
    before = jnp.cumsum(onehot, axis=0) - onehot
    order_rank = jnp.sum(before * onehot, axis=1)
    slot_index = neigh_shard * slot_cap + order_rank
    table = jnp.zeros((seq_count * slot_cap,), jnp.int32).at[slot_index].set(neigh_offset + 1)
    wanted = lax.all_to_all(
        table.reshape(seq_count, slot_cap), "seq", split_axis=0, concat_axis=0, tiled=True
    )
    first_group = jnp.maximum(wanted - 1, 0)
    stored = db_states.reshape(db_states.shape[0], -1)
    outgoing = jnp.stack(
        [jnp.take(stored, first_group, axis=0), jnp.take(stored, first_group + 1, axis=0)], axis=2
    )
    incoming = lax.all_to_all(outgoing, "seq", split_axis=0, concat_axis=0, tiled=True)
    picked = jnp.take(incoming.reshape(seq_count * slot_cap, 2, -1), slot_index, axis=0)
    enc_rows = picked.reshape(token_rows, -1)
    as_float = lax.all_gather(enc_rows, "tensor", axis=1, tiled=True).astype(jnp.float32)
    scaled = (as_float * enc_gain[None, :]).astype(jnp.bfloat16)
    kv_sum = jnp.dot(scaled, projection, preferred_element_type=jnp.float32)
    kv_sum, square_sum = (kv_sum, jnp.sum(as_float * as_float, axis=1))
    inv_rms = lax.rsqrt(square_sum / enc_width + epsilon)
    keys_values = (kv_sum * inv_rms[:, None]).astype(jnp.bfloat16)
    kv_groups = keys_values.reshape(group_count, 4 * group_len, 2, head_count, HEAD_DIM)
    previous = passed_along(kv_groups[group_count - 1], "seq", 1)
    padded = jnp.concatenate(
        [
            jnp.zeros((1, query_cols), jnp.bfloat16),
            queries,
            jnp.zeros((group_len - 1, query_cols), jnp.bfloat16),
        ],
        axis=0,
    )
    windows = padded.reshape(group_count + 1, group_len, head_count, HEAD_DIM)
    attended = attend(windows, jnp.concatenate([previous[None], kv_groups], axis=0))
    result = attended[1 : tok_count + 1]
    return result


def solution(mesh):
    return jax.shard_map(
        per_device,
        mesh=mesh,
        in_specs=(
            P("seq", "tensor"),
            P("seq", None, "tensor"),
            P(),
            P(None, None, "tensor"),
            P("seq", None),
            P("seq", None),
        ),
        out_specs=P("seq", "tensor"),
        check_vma=False,
    )
```

profile of v0, /device:TPU:0, one launch (start us, length us, event | category | flops | bytes accessed | tf_op | source)
XLA Modules:
  0.0 213.9 jit_solution(16390059754301208129)
XLA Ops:
  10.8 7.3 %all-to-all-start = ((s32[8,1,4]{2,1,0:T(1,128)}), s32[8,1,4]{2,1,0:T(1,128)S(1)}, u32[]{:S(2)}, u32[]{:S(2)}) async-start(s32[8,1,4]{2,1,0:T(1,128)} %bitcast.2), calls=%async_computation | async-start | bytes 8192 | tf_op jit(solution)/shard_map/all_to_all | solution.py:50
  18.0 1.9 reshape.89
  20.0 4.5 %all-to-all-done = s32[8,1,4]{2,1,0:T(1,128)S(1)} async-done(((s32[8,1,4]{2,1,0:T(1,128)}), s32[8,1,4]{2,1,0:T(1,128)S(1)}, u32[]{:S(2)}, u32[]{:S(2)}) %all-to-all-start) | async-done | bytes 160 | tf_op jit(solution)/shard_map/all_to_all | solution.py:50
  28.9 2.5 %pad_maximum_fusion.1 = bf16[8,4,2,14336]{3,1,2,0:T(4,128)(2,1)} fusion(bf16[8,4,1,14336]{3,1,2,0:T(4,128)(2,1)S(1)} %get-tuple-element.10, bf16[8,4,1,14336]{3,1,2,0:T(4,128)(2,1)S(1)} %get-tuple-element.11), kind=kLoop, calls=%fused_computation.27 | loop fusion | flops 917504 | bytes 3670016 | tf_op jit(solution)/shard_map/stack | solution.py:55
  31.4 3.6 %all-to-all-start.1 = ((bf16[8,4,2,14336]{3,1,2,0:T(4,128)(2,1)}), bf16[8,4,2,14336]{3,1,2,0:T(4,128)(2,1)S(1)}, u32[]{:S(2)}, u32[]{:S(2)}) async-start(bf16[8,4,2,14336]{3,1,2,0:T(4,128)(2,1)} %pad_maximum_fusion.1), calls=%async_computation.1 | async-start | bytes 3670016 | tf_op jit(solution)/shard_map/all_to_all | solution.py:58
  35.3 41.1 %all-to-all-done.1 = bf16[8,4,2,14336]{3,1,2,0:T(4,128)(2,1)S(1)} async-done(((bf16[8,4,2,14336]{3,1,2,0:T(4,128)(2,1)}), bf16[8,4,2,14336]{3,1,2,0:T(4,128)(2,1)S(1)}, u32[]{:S(2)}, u32[]{:S(2)}) %all-to-all-start.1) | async-done | bytes 1835040 | tf_op jit(solution)/shard_map/all_to_all | solution.py:58
  76.4 3.1 %copy.56 = bf16[8,4,2,14336]{3,2,1,0:T(2,128)(2,1)} copy(bf16[8,4,2,14336]{3,1,2,0:T(4,128)(2,1)S(1)} %all-to-all-done.1) | data formatting | bytes 3670016 | tf_op jit(solution)/shard_map/all_to_all | solution.py:58
  79.5 5.3 %gather_fusion = bf16[28,2,14336]{2,1,0:T(2,128)(2,1)S(1)} fusion(bf16[32,2,14336]{2,1,0:T(2,128)(2,1)} %bitcast.48, s32[1024]{0:T(1024)S(1)} %pad_clamp_fusion), kind=kCustom, calls=%fused_computation.2 | custom fusion | bytes 3211376 | tf_op jit(solution)/shard_map/jit(_take)/gather | solution.py:59
  84.8 1.5 broadcast_select_fusion
  86.3 2.6 %select_n.35 = bf16[3584,224]{1,0:T(8,128)(2,1)S(1)} reshape(bf16[28,2,14336]{2,1,0:T(2,128)(2,1)S(1)} %broadcast_select_fusion) | data formatting | bytes 3211264 | tf_op jit(solution)/shard_map/jit(_take)/select_n | solution.py:59
  89.0 2.6 %copy.57 = bf16[3584,224]{0,1:T(8,128)(2,1)} copy(bf16[3584,224]{1,0:T(8,128)(2,1)S(1)} %select_n.35) | data formatting | bytes 3211264 | tf_op jit(solution)/shard_map/jit(_take)/select_n | solution.py:59
  91.6 2.0 copy.65
  93.6 44.3 %all-gather.2.cloned.1.call-done = bf16[3584,896]{0,1:T(8,128)(2,1)} async-done(((bf16[3584,224]{0,1:T(8,128)(2,1)}), bf16[3584,896]{0,1:T(8,128)(2,1)}) %all-gather.2.cloned.1.call-update) | async-done | bytes 6422544 | tf_op jit(solution)/shard_map/all_gather | solution.py:61
  137.9 4.3 %fusion.2 = f32[3584]{0:T(1024)S(1)} fusion(bf16[3584,896]{0,1:T(8,128)(2,1)} %all-gather.2.cloned.1.call-done), kind=kLoop, calls=%fused_computation.9 | loop fusion | flops 9630208 | bytes 6436864 | tf_op jit(solution)/shard_map/reduce_sum | solution.py:64
  142.5 8.7 %multiply_convert_fusion = bf16[3584,1024]{0,1:T(8,128)(2,1)S(1)} fusion(bf16[896,1024]{1,0:T(8,128)(2,1)S(1)} %bitcast.53, f32[3584]{0:T(1024)S(1)} %add_rsqrt_fusion, bf16[3584,896]{0,1:T(8,128)(2,1)S(1)} %copy-done.1, f32[896]{0:T(1024)S(1)} %copy-done.4), kind=kOutput, calls=%fused_computation.7 | convolution fusion | flops 6593642496 | bytes 15615488 | tf_op jit(solution)/shard_map/dot_general | solution.py:63
  151.2 3.0 %copy-done = bf16[3584,1024]{0,1:T(8,128)(2,1)} copy-done((bf16[3584,1024]{0,1:T(8,128)(2,1)}, bf16[3584,1024]{0,1:T(8,128)(2,1)S(1)}, u32[]{:S(2)}) %copy-start) | copy-done | bytes 7340056
  155.2 3.4 %collective-permute-start = (bf16[256,2,4,128]{3,0,2,1:T(8,128)(2,1)}, bf16[256,2,4,128]{3,0,2,1:T(8,128)(2,1)S(1)}, u32[]{:S(2)}, u32[]{:S(2)}) collective-permute-start(bf16[256,2,4,128]{3,0,2,1:T(8,128)(2,1)} %copy.58), channel_id=1, source_target_pairs={{0,4},{4,8},{8,12},{12,16},{16,20},{20,24},{24,28},{1,5},{5,9},{9,... | collective-permute-start | bytes 1572872 | tf_op jit(solution)/shard_map/ppermute | solution.py:14
  159.4 13.7 %reshape.139 = bf16[14,256,2,4,128]{1,0,4,3,2:T(8,128)(2,1)} reshape(bf16[3584,1024]{0,1:T(8,128)(2,1)} %copy-done) | data formatting | bytes 14680064 | tf_op jit(solution)/shard_map/reshape | solution.py:67
  173.1 14.2 %copy.60 = bf16[14,256,2,4,128]{4,1,3,0,2:T(8,128)(2,1)} copy(bf16[14,256,2,4,128]{1,0,4,3,2:T(8,128)(2,1)} %reshape.139) | data formatting | bytes 14680064 | tf_op jit(solution)/shard_map/reshape | solution.py:67
  187.3 3.1 %fusion.7 = f32[15,4,64,256]{3,2,1,0:T(8,128)S(1)} fusion(bf16[1,256,2,4,128]{4,1,3,0,2:T(8,128)(2,1)S(1)} %bitcast.54, bf16[14,256,2,4,128]{4,1,3,0,2:T(8,128)(2,1)} %copy.60, bf16[15,64,4,128]{3,2,1,0:T(4,128)(2,1)S(1)} %reshape.93), kind=kOutput, calls=%fused_computation.15 | convolution fusion | flops 253624320 | bytes 12779520 | tf_op jit(solution)/shard_map/wqhd,wkhd->whqk/dot_general | solution.py:18
  190.4 1.9 copy-done.2
  192.3 1.5 fusion.39
  193.7 11.2 %fusion.21 = bf16[15,64,4,128]{3,1,2,0:T(8,128)(2,1)S(1)} fusion(bf16[14,256,2,4,128]{4,1,3,0,2:T(8,128)(2,1)} %copy.60, bf16[1,256,2,4,128]{4,1,3,0,2:T(8,128)(2,1)S(1)} %bitcast.55, f32[15,4,64]{2,1,0:T(4,128)S(1)} %fusion.39, f32[15,4,64,256]{3,2,1,0:T(8,128)} %copy-done.2), kind=kOutput, calls=%fused_computation.29 | convolution fusion | flops 264933376 | bytes 12794880 | tf_op jit(solution)/shard_map/whqk,wkhd->wqhd/dot_general | solution.py:24
  205.9 1.1 slice.26
  (53 shorter events, 12.0 us)
Async XLA Ops:
  10.8 13.6 %all-to-all-start = ((s32[8,1,4]{2,1,0:T(1,128)}), s32[8,1,4]{2,1,0:T(1,128)S(1)}, u32[]{:S(2)}, u32[]{:S(2)}) async-start(s32[8,1,4]{2,1,0:T(1,128)} %bitcast.2), calls=%async_computation | async-start | bytes 8192 | tf_op jit(solution)/shard_map/all_to_all | solution.py:50
  31.4 45.0 %all-to-all-start.1 = ((bf16[8,4,2,14336]{3,1,2,0:T(4,128)(2,1)}), bf16[8,4,2,14336]{3,1,2,0:T(4,128)(2,1)S(1)}, u32[]{:S(2)}, u32[]{:S(2)}) async-start(bf16[8,4,2,14336]{3,1,2,0:T(4,128)(2,1)} %pad_maximum_fusion.1), calls=%async_computation.1 | async-start | bytes 3670016 | tf_op jit(solution)/shard_map/all_to_all | solution.py:58
  35.0 102.9 %all-gather.2.cloned.1.call-start = ((), (), s32[]{:S(2)}) async-start(), calls=%async_computation.2 | async-start | bytes 8028160 | tf_op jit(solution)/shard_map/all_gather | solution.py:61
  93.6 48.6 %copy-start.4 = (f32[896]{0:T(1024)S(1)}, f32[896]{0:T(1024)}, u32[]{:S(2)}) copy-start(f32[896]{0:T(1024)} %param.10) | copy-start | bytes 10756
  137.9 4.7 %copy-start.1 = (bf16[3584,896]{0,1:T(8,128)(2,1)S(1)}, bf16[3584,896]{0,1:T(8,128)(2,1)}, u32[]{:S(2)}) copy-start(bf16[3584,896]{0,1:T(8,128)(2,1)} %all-gather.2.cloned.1.call-done) | copy-start | bytes 19267588
  142.5 16.2 %copy-start.3 = (bf16[896,512]{1,0:T(8,128)(2,1)S(1)}, bf16[896,512]{1,0:T(8,128)(2,1)}, u32[]{:S(2)}) copy-start(bf16[896,512]{1,0:T(8,128)(2,1)} %param.8) | copy-start | bytes 2752516
  151.2 3.0 %copy-start = (bf16[3584,1024]{0,1:T(8,128)(2,1)}, bf16[3584,1024]{0,1:T(8,128)(2,1)S(1)}, u32[]{:S(2)}) copy-start(bf16[3584,1024]{0,1:T(8,128)(2,1)S(1)} %multiply_convert_fusion) | copy-start | bytes 22020100
  155.2 32.0 %collective-permute-start = (bf16[256,2,4,128]{3,0,2,1:T(8,128)(2,1)}, bf16[256,2,4,128]{3,0,2,1:T(8,128)(2,1)S(1)}, u32[]{:S(2)}, u32[]{:S(2)}) collective-permute-start(bf16[256,2,4,128]{3,0,2,1:T(8,128)(2,1)} %copy.58), channel_id=1, source_target_pairs={{0,4},{4,8},{8,12},{12,16},{16,20},{20,24},{24,28},{1,5},{5,9},{9,... | collective-permute-start | bytes 1572872 | tf_op jit(solution)/shard_map/ppermute | solution.py:14
  190.4 1.9 copy-start.2
Sparse Core Ops, SparseCore 0:
  91.7 46.1 all-gather.1
where the time goes:
time: 215 us; the launch traced here: 214 us
  waiting for transfers between devices  89.9 us (42%)
  local copies, waits for them, and re-layouts  60.2 us (28%)
  matrix products  23 us (11%)
  starting transfers between devices  14.4 us (7%)
  between operations  13.6 us (6%)
  other arithmetic  12.7 us (6%)
    all_gather x1, waiting for transfers between devices, per_device(): lax.all_gather(enc_rows, 'tensor', axis=1, tiled=True).astype(jnp.float32)  44.3 us
    all_to_all x1, waiting for transfers between devices, per_device(): lax.all_to_all(outgoing, 'seq', split_axis=0, concat_axis=0, tiled=True)  41.1 us
    reshape x2, local copies, waits for them, and re-layouts, per_device(): keys_values.reshape(group_count, 4 * group_len, 2, head_count, HEAD_DIM)  27.9 us
    dot_general x1, matrix products, attend(): jnp.einsum('whqk,wkhd->wqhd', weights, kv_win[:, :, 1], preferred_element...  11.2 us
    dot_general x1, matrix products, per_device(): kv_sum = jnp.dot(scaled, projection, preferred_element_type=jnp.float32)  8.67 us
    unnamed x13, local copies, waits for them, and re-layouts  8.17 us
    all_to_all x1, starting transfers between devices, per_device(): lax.all_to_all(table.reshape(seq_count, slot_cap), 'seq', split_axis=0, c...  7.25 us
    gather x1, local copies, waits for them, and re-layouts, per_device(): jnp.take(incoming.reshape(seq_count * slot_cap, 2, -1), slot_index, axis=0)  5.28 us
  transfers between devices with their start and end apart: 4, of which 3 were waited for; matrix products, arithmetic and copies ran while one was open for 15% of the time, Pallas kernels for 0%

commit v1 on v0

--- a/solution.py
+++ b/solution.py
@@ -55,7 +55,19 @@
     outgoing = jnp.stack(
         [jnp.take(stored, first_group, axis=0), jnp.take(stored, first_group + 1, axis=0)], axis=2
     )
-    incoming = lax.all_to_all(outgoing, "seq", split_axis=0, concat_axis=0, tiled=True)
+    ways, here = (lax.axis_size("seq"), lax.axis_index("seq"))
+    width = outgoing.shape[0] // ways
+    shape = list(outgoing.shape)
+    shape[0] = width
+    height = shape[0]
+    shape[0] = height * ways
+    full = jnp.zeros(shape, outgoing.dtype)
+    for mask in range(ways):
+        part = lax.dynamic_slice_in_dim(outgoing, (here ^ mask) * width, width, axis=0)
+        if mask:
+            part = lax.ppermute(part, "seq", [(d, d ^ mask) for d in range(ways)])
+        full = lax.dynamic_update_slice_in_dim(full, part, (here ^ mask) * height, axis=0)
+    incoming = full
     picked = jnp.take(incoming.reshape(seq_count * slot_cap, 2, -1), slot_index, axis=0)
     enc_rows = picked.reshape(token_rows, -1)
     as_float = lax.all_gather(enc_rows, "tensor", axis=1, tiled=True).astype(jnp.float32)

time: 215 us -> 207 us (0.963)
  waiting for transfers between devices: 89.9 us -> 71 us
  starting transfers between devices: 14.4 us -> 24.8 us
    all_to_all x1 -> x0, waiting for transfers between devices: 41.1 us -> none  [per_device(): lax.all_to_all(outgoing, 'seq', split_axis=0, concat_axis=0, tiled=True)]
    ppermute x0 -> x7, waiting for transfers between devices: none -> 23.2 us  [per_device(): part = lax.ppermute(part, 'seq', [(d, d ^ mask) for d in range(ways)])]
    ppermute x0 -> x7, starting transfers between devices: none -> 13.9 us  [per_device(): part = lax.ppermute(part, 'seq', [(d, d ^ mask) for d in range(ways)])]
    all_to_all x1 -> x0, starting transfers between devices: 3.59 us -> none  [per_device(): lax.all_to_all(outgoing, 'seq', split_axis=0, concat_axis=0, tiled=True)]
    all_to_all x1 -> x0, local copies, waits for them, and re-layouts: 3.14 us -> none  [per_device(): lax.all_to_all(outgoing, 'seq', split_axis=0, concat_axis=0, tiled=True)]
  transfers between devices with their start and end apart: 4 -> 10, of which waited for: 3 -> 6; matrix products, arithmetic and copies ran while one was open for 15% -> 18% of each run, Pallas kernels for 0% -> 0%
where the time goes in v1:
time: 207 us; the launch traced here: 206 us
  waiting for transfers between devices  71 us (34%)
  local copies, waits for them, and re-layouts  60.7 us (29%)
  starting transfers between devices  24.8 us (12%)
  matrix products  22.9 us (11%)
  between operations  13.8 us (7%)
  other arithmetic  12.8 us (6%)
    all_gather x1, waiting for transfers between devices, per_device(): lax.all_gather(enc_rows, 'tensor', axis=1, tiled=True).astype(jnp.float32)  43.5 us
    reshape x2, local copies, waits for them, and re-layouts, per_device(): keys_values.reshape(group_count, 4 * group_len, 2, head_count, HEAD_DIM)  27.6 us
    ppermute x7, waiting for transfers between devices, per_device(): part = lax.ppermute(part, 'seq', [(d, d ^ mask) for d in range(ways)])  23.2 us
    ppermute x7, starting transfers between devices, per_device(): part = lax.ppermute(part, 'seq', [(d, d ^ mask) for d in range(ways)])  13.9 us
    dot_general x1, matrix products, attend(): jnp.einsum('whqk,wkhd->wqhd', weights, kv_win[:, :, 1], preferred_element...  11.2 us
    dot_general x1, matrix products, per_device(): kv_sum = jnp.dot(scaled, projection, preferred_element_type=jnp.float32)  8.67 us
    unnamed x13, local copies, waits for them, and re-layouts  8.14 us
    select_n x2, local copies, waits for them, and re-layouts, per_device(): jnp.take(incoming.reshape(seq_count * slot_cap, 2, -1), slot_index, axis=0)  7.28 us
  transfers between devices with their start and end apart: 10, of which 6 were waited for; matrix products, arithmetic and copies ran while one was open for 18% of the time, Pallas kernels for 0%

profile of v1, /device:TPU:0, one launch (start us, length us, event | category | flops | bytes accessed | tf_op | source)
XLA Modules:
  0.0 206.0 jit_solution(6116577742345557067)
XLA Ops:
  10.8 7.3 %all-to-all-start = ((s32[8,1,4]{2,1,0:T(1,128)}), s32[8,1,4]{2,1,0:T(1,128)S(1)}, u32[]{:S(2)}, u32[]{:S(2)}) async-start(s32[8,1,4]{2,1,0:T(1,128)} %bitcast.2), calls=%async_computation | async-start | bytes 8192 | tf_op jit(solution)/shard_map/all_to_all | solution.py:50
  18.1 1.9 reshape.89
  20.1 4.3 %all-to-all-done = s32[8,1,4]{2,1,0:T(1,128)S(1)} async-done(((s32[8,1,4]{2,1,0:T(1,128)}), s32[8,1,4]{2,1,0:T(1,128)S(1)}, u32[]{:S(2)}, u32[]{:S(2)}) %all-to-all-start) | async-done | bytes 160 | tf_op jit(solution)/shard_map/all_to_all | solution.py:50
  32.4 2.4 %collective-permute-start.6 = (bf16[1,4,2,14336]{3,1,0,2:T(4,128)(2,1)S(1)}, bf16[1,4,2,14336]{3,1,0,2:T(4,128)(2,1)S(1)}, u32[]{:S(2)}, u32[]{:S(2)}) collective-permute-start(bf16[1,4,2,14336]{3,1,0,2:T(4,128)(2,1)S(1)} %get-tuple-element.6), channel_id=1, source_target_pairs={{0,28},{4,24},{8,20},{12,16},{16,12},{20,8},{24,4},{28,0},{1,29},{... | collective-permute-start | bytes 688136 | tf_op jit(solution)/shard_map/ppermute | solution.py:68
  37.8 4.4 %collective-permute-done = bf16[1,4,2,14336]{3,1,0,2:T(4,128)(2,1)S(1)} collective-permute-done((bf16[1,4,2,14336]{3,1,0,2:T(4,128)(2,1)S(1)}, bf16[1,4,2,14336]{3,1,0,2:T(4,128)(2,1)S(1)}, u32[]{:S(2)}, u32[]{:S(2)}) %collective-permute-start) | collective-permute-done | bytes 229408 | tf_op jit(solution)/shard_map/ppermute | solution.py:68
  42.3 3.6 %collective-permute-start.2 = (bf16[1,4,2,14336]{3,1,0,2:T(4,128)(2,1)S(1)}, bf16[1,4,2,14336]{3,1,0,2:T(4,128)(2,1)S(1)}, u32[]{:S(2)}, u32[]{:S(2)}) collective-permute-start(bf16[1,4,2,14336]{3,1,0,2:T(4,128)(2,1)S(1)} %get-tuple-element.10), channel_id=1, source_target_pairs={{0,12},{4,8},{8,4},{12,0},{16,28},{20,24},{24,20},{28,16},{1,13},{... | collective-permute-start | bytes 688136 | tf_op jit(solution)/shard_map/ppermute | solution.py:68
  46.1 4.6 %collective-permute-done.1 = bf16[1,4,2,14336]{3,1,0,2:T(4,128)(2,1)S(1)} collective-permute-done((bf16[1,4,2,14336]{3,1,0,2:T(4,128)(2,1)S(1)}, bf16[1,4,2,14336]{3,1,0,2:T(4,128)(2,1)S(1)}, u32[]{:S(2)}, u32[]{:S(2)}) %collective-permute-start.1) | collective-permute-done | bytes 229408 | tf_op jit(solution)/shard_map/ppermute | solution.py:68
  50.7 4.3 %collective-permute-start.3 = (bf16[1,4,2,14336]{3,1,0,2:T(4,128)(2,1)S(1)}, bf16[1,4,2,14336]{3,1,0,2:T(4,128)(2,1)S(1)}, u32[]{:S(2)}, u32[]{:S(2)}) collective-permute-start(bf16[1,4,2,14336]{3,1,0,2:T(4,128)(2,1)S(1)} %get-tuple-element.11), channel_id=1, source_target_pairs={{0,16},{4,20},{8,24},{12,28},{16,0},{20,4},{24,8},{28,12},{1,17},{... | collective-permute-start | bytes 688136 | tf_op jit(solution)/shard_map/ppermute | solution.py:68
  57.2 12.4 %collective-permute-done.3 = bf16[1,4,2,14336]{3,1,0,2:T(4,128)(2,1)S(1)} collective-permute-done((bf16[1,4,2,14336]{3,1,0,2:T(4,128)(2,1)S(1)}, bf16[1,4,2,14336]{3,1,0,2:T(4,128)(2,1)S(1)}, u32[]{:S(2)}, u32[]{:S(2)}) %collective-permute-start.3) | collective-permute-done | bytes 229408 | tf_op jit(solution)/shard_map/ppermute | solution.py:68
  70.7 4.0 %gather_fusion = bf16[28,2,14336]{2,1,0:T(2,128)(2,1)S(1)} fusion(bf16[32,2,14336]{2,1,0:T(2,128)(2,1)S(1)} %bitcast.48, s32[1024]{0:T(1024)S(1)} %pad_clamp_fusion), kind=kCustom, calls=%fused_computation.2 | custom fusion | bytes 3211376 | tf_op jit(solution)/shard_map/jit(_take)/gather | solution.py:71
  74.7 2.7 %broadcast_select_fusion = bf16[28,2,14336]{2,1,0:T(2,128)(2,1)} fusion(bf16[28,2,14336]{2,1,0:T(2,128)(2,1)S(1)} %gather_fusion, pred[28]{0:T(512)(128)(4,1)S(1)} %compare_and_fusion.2), kind=kLoop, calls=%fused_computation.24 | loop fusion | flops 802816 | bytes 3211292 | tf_op jit(solution)/shard_map/jit(_take)/select_n | solution.py:71
  77.3 4.7 %select_n.75 = bf16[3584,224]{1,0:T(8,128)(2,1)S(1)} reshape(bf16[28,2,14336]{2,1,0:T(2,128)(2,1)} %broadcast_select_fusion) | data formatting | bytes 3211264 | tf_op jit(solution)/shard_map/jit(_take)/select_n | solution.py:71
  82.0 2.6 %copy.78 = bf16[3584,224]{0,1:T(8,128)(2,1)} copy(bf16[3584,224]{1,0:T(8,128)(2,1)S(1)} %select_n.75) | data formatting | bytes 3211264 | tf_op jit(solution)/shard_map/jit(_take)/select_n | solution.py:71
  84.6 2.0 copy.86
  86.6 43.5 %all-gather.2.cloned.1.call-done = bf16[3584,896]{0,1:T(8,128)(2,1)} async-done(((bf16[3584,224]{0,1:T(8,128)(2,1)}), bf16[3584,896]{0,1:T(8,128)(2,1)}) %all-gather.2.cloned.1.call-update) | async-done | bytes 6422544 | tf_op jit(solution)/shard_map/all_gather | solution.py:73
  130.1 4.3 %fusion.2 = f32[3584]{0:T(1024)S(1)} fusion(bf16[3584,896]{0,1:T(8,128)(2,1)} %all-gather.2.cloned.1.call-done), kind=kLoop, calls=%fused_computation.9 | loop fusion | flops 9630208 | bytes 6436864 | tf_op jit(solution)/shard_map/reduce_sum | solution.py:76
  134.8 8.7 %multiply_convert_fusion = bf16[3584,1024]{0,1:T(8,128)(2,1)S(1)} fusion(bf16[896,1024]{1,0:T(8,128)(2,1)S(1)} %bitcast.53, f32[3584]{0:T(1024)S(1)} %add_rsqrt_fusion, bf16[3584,896]{0,1:T(8,128)(2,1)S(1)} %copy-done.1, f32[896]{0:T(1024)S(1)} %copy-done.4), kind=kOutput, calls=%fused_computation.7 | convolution fusion | flops 6593642496 | bytes 15615488 | tf_op jit(solution)/shard_map/dot_general | solution.py:75
  143.5 3.0 %copy-done = bf16[3584,1024]{0,1:T(8,128)(2,1)} copy-done((bf16[3584,1024]{0,1:T(8,128)(2,1)}, bf16[3584,1024]{0,1:T(8,128)(2,1)S(1)}, u32[]{:S(2)}) %copy-start) | copy-done | bytes 7340056
  147.5 3.6 %collective-permute-start.7 = (bf16[256,2,4,128]{3,0,2,1:T(8,128)(2,1)}, bf16[256,2,4,128]{3,0,2,1:T(8,128)(2,1)S(1)}, u32[]{:S(2)}, u32[]{:S(2)}) collective-permute-start(bf16[256,2,4,128]{3,0,2,1:T(8,128)(2,1)} %copy.79), channel_id=1, source_target_pairs={{0,4},{4,8},{8,12},{12,16},{16,20},{20,24},{24,28},{1,5},{5,9},{9,... | collective-permute-start | bytes 1572872 | tf_op jit(solution)/shard_map/ppermute | solution.py:14
  151.8 13.5 %reshape.139 = bf16[14,256,2,4,128]{1,0,4,3,2:T(8,128)(2,1)} reshape(bf16[3584,1024]{0,1:T(8,128)(2,1)} %copy-done) | data formatting | bytes 14680064 | tf_op jit(solution)/shard_map/reshape | solution.py:79
  165.3 14.2 %copy.81 = bf16[14,256,2,4,128]{4,1,3,0,2:T(8,128)(2,1)} copy(bf16[14,256,2,4,128]{1,0,4,3,2:T(8,128)(2,1)} %reshape.139) | data formatting | bytes 14680064 | tf_op jit(solution)/shard_map/reshape | solution.py:79
  179.5 3.1 %fusion.7 = f32[15,4,64,256]{3,2,1,0:T(8,128)S(1)} fusion(bf16[1,256,2,4,128]{4,1,3,0,2:T(8,128)(2,1)S(1)} %bitcast.54, bf16[14,256,2,4,128]{4,1,3,0,2:T(8,128)(2,1)} %copy.81, bf16[15,64,4,128]{3,2,1,0:T(4,128)(2,1)S(1)} %reshape.93), kind=kOutput, calls=%fused_computation.15 | convolution fusion | flops 253624320 | bytes 12779520 | tf_op jit(solution)/shard_map/wqhd,wkhd->whqk/dot_general | solution.py:18
  182.6 1.8 copy-done.2
  185.9 11.2 %fusion.21 = bf16[15,64,4,128]{3,1,2,0:T(8,128)(2,1)S(1)} fusion(bf16[14,256,2,4,128]{4,1,3,0,2:T(8,128)(2,1)} %copy.81, bf16[1,256,2,4,128]{4,1,3,0,2:T(8,128)(2,1)S(1)} %bitcast.55, f32[15,4,64]{2,1,0:T(4,128)S(1)} %fusion.47, f32[15,4,64,256]{3,2,1,0:T(8,128)} %copy-done.2), kind=kOutput, calls=%fused_computation.44 | convolution fusion | flops 264933376 | bytes 12794880 | tf_op jit(solution)/shard_map/whqk,wkhd->wqhd/dot_general | solution.py:24
  (74 shorter events, 24.5 us)
Async XLA Ops:
  10.8 13.6 %all-to-all-start = ((s32[8,1,4]{2,1,0:T(1,128)}), s32[8,1,4]{2,1,0:T(1,128)S(1)}, u32[]{:S(2)}, u32[]{:S(2)}) async-start(s32[8,1,4]{2,1,0:T(1,128)} %bitcast.2), calls=%async_computation | async-start | bytes 8192 | tf_op jit(solution)/shard_map/all_to_all | solution.py:50
  18.0 112.1 %all-gather.2.cloned.1.call-start = ((), (), s32[]{:S(2)}) async-start(), calls=%async_computation.1 | async-start | bytes 8028160 | tf_op jit(solution)/shard_map/all_gather | solution.py:73
  29.2 40.9 %collective-permute-start.5 = (bf16[1,4,2,14336]{3,1,0,2:T(4,128)(2,1)S(1)}, bf16[1,4,2,14336]{3,1,0,2:T(4,128)(2,1)S(1)}, u32[]{:S(2)}, u32[]{:S(2)}) collective-permute-start(bf16[1,4,2,14336]{3,1,0,2:T(4,128)(2,1)S(1)} %get-tuple-element.12), channel_id=1, source_target_pairs={{0,24},{4,28},{8,16},{12,20},{16,8},{20,12},{24,0},{28,4},{1,25},{... | collective-permute-start | bytes 688136 | tf_op jit(solution)/shard_map/ppermute | solution.py:68
  29.9 40.0 %collective-permute-start.4 = (bf16[1,4,2,14336]{3,1,0,2:T(4,128)(2,1)S(1)}, bf16[1,4,2,14336]{3,1,0,2:T(4,128)(2,1)S(1)}, u32[]{:S(2)}, u32[]{:S(2)}) collective-permute-start(bf16[1,4,2,14336]{3,1,0,2:T(4,128)(2,1)S(1)} %get-tuple-element.13), channel_id=1, source_target_pairs={{0,20},{4,16},{8,28},{12,24},{16,4},{20,0},{24,12},{28,8},{1,21},{... | collective-permute-start | bytes 688136 | tf_op jit(solution)/shard_map/ppermute | solution.py:68
  32.4 38.0 %collective-permute-start.6 = (bf16[1,4,2,14336]{3,1,0,2:T(4,128)(2,1)S(1)}, bf16[1,4,2,14336]{3,1,0,2:T(4,128)(2,1)S(1)}, u32[]{:S(2)}, u32[]{:S(2)}) collective-permute-start(bf16[1,4,2,14336]{3,1,0,2:T(4,128)(2,1)S(1)} %get-tuple-element.6), channel_id=1, source_target_pairs={{0,28},{4,24},{8,20},{12,16},{16,12},{20,8},{24,4},{28,0},{1,29},{... | collective-permute-start | bytes 688136 | tf_op jit(solution)/shard_map/ppermute | solution.py:68
  34.8 7.4 %collective-permute-start = (bf16[1,4,2,14336]{3,1,0,2:T(4,128)(2,1)S(1)}, bf16[1,4,2,14336]{3,1,0,2:T(4,128)(2,1)S(1)}, u32[]{:S(2)}, u32[]{:S(2)}) collective-permute-start(bf16[1,4,2,14336]{3,1,0,2:T(4,128)(2,1)S(1)} %get-tuple-element.8), channel_id=1, source_target_pairs={{0,4},{4,0},{8,12},{12,8},{16,20},{20,16},{24,28},{28,24},{1,5},{5... | collective-permute-start | bytes 688136 | tf_op jit(solution)/shard_map/ppermute | solution.py:68
  35.8 14.9 %collective-permute-start.1 = (bf16[1,4,2,14336]{3,1,0,2:T(4,128)(2,1)S(1)}, bf16[1,4,2,14336]{3,1,0,2:T(4,128)(2,1)S(1)}, u32[]{:S(2)}, u32[]{:S(2)}) collective-permute-start(bf16[1,4,2,14336]{3,1,0,2:T(4,128)(2,1)S(1)} %get-tuple-element.9), channel_id=1, source_target_pairs={{0,8},{4,12},{8,0},{12,4},{16,24},{20,28},{24,16},{28,20},{1,9},{5... | collective-permute-start | bytes 688136 | tf_op jit(solution)/shard_map/ppermute | solution.py:68
  42.3 14.7 %collective-permute-start.2 = (bf16[1,4,2,14336]{3,1,0,2:T(4,128)(2,1)S(1)}, bf16[1,4,2,14336]{3,1,0,2:T(4,128)(2,1)S(1)}, u32[]{:S(2)}, u32[]{:S(2)}) collective-permute-start(bf16[1,4,2,14336]{3,1,0,2:T(4,128)(2,1)S(1)} %get-tuple-element.10), channel_id=1, source_target_pairs={{0,12},{4,8},{8,4},{12,0},{16,28},{20,24},{24,20},{28,16},{1,13},{... | collective-permute-start | bytes 688136 | tf_op jit(solution)/shard_map/ppermute | solution.py:68
  50.7 18.9 %collective-permute-start.3 = (bf16[1,4,2,14336]{3,1,0,2:T(4,128)(2,1)S(1)}, bf16[1,4,2,14336]{3,1,0,2:T(4,128)(2,1)S(1)}, u32[]{:S(2)}, u32[]{:S(2)}) collective-permute-start(bf16[1,4,2,14336]{3,1,0,2:T(4,128)(2,1)S(1)} %get-tuple-element.11), channel_id=1, source_target_pairs={{0,16},{4,20},{8,24},{12,28},{16,0},{20,4},{24,8},{28,12},{1,17},{... | collective-permute-start | bytes 688136 | tf_op jit(solution)/shard_map/ppermute | solution.py:68
  86.6 47.8 %copy-start.4 = (f32[896]{0:T(1024)S(1)}, f32[896]{0:T(1024)}, u32[]{:S(2)}) copy-start(f32[896]{0:T(1024)} %param.10) | copy-start | bytes 10756
  130.1 4.7 %copy-start.1 = (bf16[3584,896]{0,1:T(8,128)(2,1)S(1)}, bf16[3584,896]{0,1:T(8,128)(2,1)}, u32[]{:S(2)}) copy-start(bf16[3584,896]{0,1:T(8,128)(2,1)} %all-gather.2.cloned.1.call-done) | copy-start | bytes 19267588
  143.5 3.0 %copy-start = (bf16[3584,1024]{0,1:T(8,128)(2,1)}, bf16[3584,1024]{0,1:T(8,128)(2,1)S(1)}, u32[]{:S(2)}) copy-start(bf16[3584,1024]{0,1:T(8,128)(2,1)S(1)} %multiply_convert_fusion) | copy-start | bytes 22020100
  146.5 4.7 %copy-start.3 = (bf16[896,512]{1,0:T(8,128)(2,1)S(1)}, bf16[896,512]{1,0:T(8,128)(2,1)}, u32[]{:S(2)}) copy-start(bf16[896,512]{1,0:T(8,128)(2,1)} %param.8) | copy-start | bytes 2752516
  147.5 32.0 %collective-permute-start.7 = (bf16[256,2,4,128]{3,0,2,1:T(8,128)(2,1)}, bf16[256,2,4,128]{3,0,2,1:T(8,128)(2,1)S(1)}, u32[]{:S(2)}, u32[]{:S(2)}) collective-permute-start(bf16[256,2,4,128]{3,0,2,1:T(8,128)(2,1)} %copy.79), channel_id=1, source_target_pairs={{0,4},{4,8},{8,12},{12,16},{16,20},{20,24},{24,28},{1,5},{5,9},{9,... | collective-permute-start | bytes 1572872 | tf_op jit(solution)/shard_map/ppermute | solution.py:14
  182.6 1.9 copy-start.2
Sparse Core Ops, SparseCore 0:
  84.7 45.3 all-gather.1
